TPU v7x, 32 devices: a whole 2x2x4 slice. The times are simulated.
32 devices in a mesh: groups: 2 (over y), mp: 4 (over z), dp: 2 (over x), rep: 2 (over core).
Axes of the slice: x: 2, y: 2, z: 4, core: 2. Of those that a mesh axis runs over, the one named last changes fastest.
Arguments:
- activations: bfloat16 [2048, 2048], P(('groups', 'dp', 'rep'), 'mp'), parts along dimension 0, may hold values from -6 to 6
- out_grads: bfloat16 [2048, 7168], P(('groups', 'dp', 'rep'), 'mp'), parts along dimension 0, may hold values from -6 to 6
- basis_grad: bfloat16 [14336, 7168], P(('groups', 'mp'), ('dp', 'rep')), parts along dimension 0, may hold values from -0.0625 to 0.0625
- basis_act: bfloat16 [4096, 2048], P(('groups', 'dp', 'rep'), 'mp'), parts along dimension 0, may hold values from -0.125 to 0.125
- eigen_values: float32 [14336, 2048], P(('groups', 'dp', 'rep'), 'mp'), parts along dimension 0, may hold values from 0.5 to 16
- token_counts: int32 [64], P(('groups', 'dp', 'rep')), parts along dimension 0, may hold values from 16 to 32
- fail_ids: int32 [48], P('groups'), parts along dimension 0, may hold values from 0 to 31, as said below
Outputs:
- preconditioned: float32 [14336, 2048], P(('groups', 'mp'), ('dp', 'rep')), parts along dimension 0
There are 2 independent parts, one for each index of `groups`. A program takes and returns all parts, laid end to end along the dimension named above; each array names one. Nothing has to cross between parts.
Inputs may be any that keep to these rules, and one draw needn't show every extreme that they name: `fail_ids`: 24 distinct prompt indices.
All inputs are finite; a program needn't handle non-finite values.
Results may differ from a plain program's by a relative error of at most 0.015.
Values may be sent and summed in bfloat16 or wider, within the bound.
A program may use at most 128 MiB of HBM per device.

v0:
```python
import jax
import jax.numpy as jnp
from jax import lax
from jax.sharding import PartitionSpec as P

LEN = 32


DAMPING = 0.25


def shards(activations, out_grads, basis_grad, basis_act, eigen_values, token_counts, fail_ids):
    prompts = token_counts.shape[0]
    token_rows = activations.shape[0]
    first_prompt = lax.axis_index(("dp", "rep")) * prompts
    prompt_index = first_prompt + jnp.arange(prompts, dtype=jnp.int32)
    chosen = jnp.any(prompt_index[:, None] == fail_ids[None, :], axis=1)
    live_slot = jnp.arange(LEN, dtype=jnp.int32)[None, :] < token_counts[:, None]
    inverse = 1.0 / token_counts.astype(jnp.float32)
    weight = jnp.where(live_slot & chosen[:, None], inverse[:, None], jnp.float32(0.0)).reshape(
        token_rows
    )
    scaled_grads = (out_grads.astype(jnp.float32) * weight[:, None]).astype(jnp.bfloat16)
    features = lax.all_gather(activations, "mp", axis=1, tiled=True)
    basis_columns = lax.all_gather(basis_act, ("dp", "rep"), axis=0, tiled=True)
    rotated = jnp.dot(features, basis_columns, preferred_element_type=jnp.float32).astype(
        jnp.bfloat16
    )
    partial_grad = lax.dot_general(
        scaled_grads,
        lax.all_gather(rotated, "mp", axis=1, tiled=True),
        (((0,), (0,)), ((), ())),
        preferred_element_type=jnp.float32,
    )
    grad_block = lax.psum_scatter(
        partial_grad.astype(jnp.bfloat16), ("dp", "rep"), scatter_dimension=1, tiled=True
    )
    partial_eigen = lax.dot_general(
        basis_grad,
        lax.all_gather(grad_block, ("dp", "rep"), axis=1, tiled=True),
        (((0,), (0,)), ((), ())),
        preferred_element_type=jnp.float32,
    )
    eigen_grad = lax.psum_scatter(
        partial_eigen.astype(jnp.bfloat16), "mp", scatter_dimension=1, tiled=True
    ).astype(jnp.float32)
    damped = (eigen_grad / (eigen_values + DAMPING)).astype(jnp.bfloat16)
    partial_back = jnp.dot(
        basis_grad,
        lax.all_gather(damped, "mp", axis=1, tiled=True),
        preferred_element_type=jnp.float32,
    )
    back_rotated = lax.psum(partial_back.astype(jnp.bfloat16), ("dp", "rep"))
    basis_rows = lax.all_gather(basis_act, "mp", axis=1, tiled=True)
    return lax.dot_general(
        back_rotated, basis_rows, (((1,), (1,)), ((), ())), preferred_element_type=jnp.float32
    )


def solution(mesh):
    return jax.shard_map(
        shards,
        mesh=mesh,
        in_specs=(
            P(("groups", "dp", "rep"), "mp"),
            P(("groups", "dp", "rep"), "mp"),
            P(("groups", "mp"), ("dp", "rep")),
            P(("groups", "dp", "rep"), "mp"),
            P(("groups", "dp", "rep"), "mp"),
            P(("groups", "dp", "rep")),
            P("groups"),
        ),
        out_specs=P(("groups", "mp"), ("dp", "rep")),
        check_vma=False,
    )
```

profile of v0, /device:TPU:0, one launch (start us, length us, event | category | flops | bytes accessed | tf_op | source)
XLA Modules:
  0.0 705.4 jit_solution(13361595270410938462)
XLA Ops:
  6.5 0.0 all-gather.7.cloned.1.call-start
  6.5 0.7 all-gather.7.cloned.1.call-update
  7.3 0.0 all-gather.9.cloned.1.call-start
  7.3 0.7 all-gather.9.cloned.1.call-update
  8.0 0.0 all-gather.11.cloned.1.call-start
  8.1 31.5 %all-gather.7.cloned.1.call-done = bf16[256,2048]{1,0:T(8,128)(2,1)} async-done(((bf16[256,512]{1,0:T(8,128)(2,1)}), bf16[256,2048]{1,0:T(8,128)(2,1)}) %all-gather.7.cloned.1.call-update) | async-done | bytes 1048592 | tf_op jit(solution)/shard_map/all_gather | solution.py:24
  39.6 23.7 %all-gather.9.cloned.1.call-done = bf16[2048,512]{1,0:T(8,128)(2,1)} async-done(((bf16[512,512]{1,0:T(8,128)(2,1)}), bf16[2048,512]{1,0:T(8,128)(2,1)}) %all-gather.9.cloned.1.call-update) | async-done | bytes 2097168 | tf_op jit(solution)/shard_map/all_gather | solution.py:25
  63.3 3.3 convolution_convert_fusion.3
  66.6 0.0 all-gather.11.cloned.1.call-update
  66.6 0.0 reduce-scatter.3.cloned.1.call-start
  66.7 0.8 compare_reduce_fusion
  67.5 0.7 convert_divide_fusion
  68.2 0.7 fusion.4
  68.9 0.1 select_n.12
  69.0 25.7 %all-gather.11.cloned.1.call-done = bf16[256,2048]{1,0:T(8,128)(2,1)} async-done(((bf16[256,512]{1,0:T(8,128)(2,1)}), bf16[256,2048]{1,0:T(8,128)(2,1)}) %all-gather.11.cloned.1.call-update) | async-done | bytes 1048592 | tf_op jit(solution)/shard_map/all_gather | solution.py:31
  94.7 6.6 convolution_convert_fusion
  101.3 0.0 reduce-scatter.3.cloned.1.call-update
  101.4 0.0 all-gather.13.cloned.1.call-start
  101.4 65.1 %reduce-scatter.3.cloned.1.call-done = bf16[1792,512]{1,0:T(8,128)(2,1)} async-done(((bf16[1792,2048]{1,0:T(8,128)(2,1)}), bf16[1792,512]{1,0:T(8,128)(2,1)}) %reduce-scatter.3.cloned.1.call-update) | async-done | bytes 1835024 | tf_op jit(solution)/shard_map/reduce_scatter | solution.py:35
  166.5 0.0 all-gather.13.cloned.1.call-update
  166.5 0.0 reduce-scatter.5.cloned.1.call-start
  166.6 53.8 %all-gather.13.cloned.1.call-done = bf16[1792,2048]{1,0:T(8,128)(2,1)} async-done(((bf16[1792,512]{1,0:T(8,128)(2,1)}), bf16[1792,2048]{1,0:T(8,128)(2,1)}) %all-gather.13.cloned.1.call-update) | async-done | bytes 7340048 | tf_op jit(solution)/shard_map/all_gather | solution.py:40
  220.4 19.6 %fusion = bf16[1792,2048]{1,0:T(8,128)(2,1)} fusion(bf16[1792,2048]{1,0:T(8,128)(2,1)} %all-gather.13.cloned.1.call-done, bf16[1792,1792]{1,0:T(8,128)(2,1)} %param.9), kind=kOutput, calls=%fused_computation.3 | convolution fusion | flops 13157007360 | bytes 21102592 | tf_op jit(solution)/shard_map/dot_general | solution.py:38
  239.9 0.0 reduce-scatter.5.cloned.1.call-update
  239.9 0.0 all-gather.15.cloned.1.call-start
  240.0 127.9 %reduce-scatter.5.cloned.1.call-done = bf16[1792,512]{1,0:T(8,128)(2,1)} async-done(((bf16[1792,2048]{1,0:T(8,128)(2,1)}), bf16[1792,512]{1,0:T(8,128)(2,1)}) %reduce-scatter.5.cloned.1.call-update) | async-done | bytes 1835024 | tf_op jit(solution)/shard_map/reduce_scatter | solution.py:44
  367.9 4.6 divide_convert_fusion
  372.5 0.0 all-gather.15.cloned.1.call-update
  372.5 0.0 all-gather.17.cloned.1.call-start
  372.5 0.7 all-gather.17.cloned.1.call-update
  373.2 0.2 all-reduce.2.cloned.1.call-start
  373.5 132.2 %all-gather.15.cloned.1.call-done = bf16[1792,2048]{1,0:T(8,128)(2,1)} async-done(((bf16[1792,512]{1,0:T(8,128)(2,1)}), bf16[1792,2048]{1,0:T(8,128)(2,1)}) %all-gather.15.cloned.1.call-update) | async-done | bytes 7340048 | tf_op jit(solution)/shard_map/all_gather | solution.py:50
  505.7 19.5 %fusion.1 = bf16[1792,2048]{0,1:T(8,128)(2,1)} fusion(bf16[1792,2048]{1,0:T(8,128)(2,1)} %all-gather.15.cloned.1.call-done, bf16[1792,1792]{1,0:T(8,128)(2,1)} %param.9), kind=kOutput, calls=%fused_computation.4 | convolution fusion | flops 13157007360 | bytes 21102592 | tf_op jit(solution)/shard_map/dot_general | solution.py:48
  525.2 0.0 all-reduce.2.cloned.1.call-update
  525.2 26.3 %all-gather.17.cloned.1.call-done = bf16[512,2048]{1,0:T(8,128)(2,1)} async-done(((bf16[512,512]{1,0:T(8,128)(2,1)}), bf16[512,2048]{1,0:T(8,128)(2,1)}) %all-gather.17.cloned.1.call-update) | async-done | bytes 2097168 | tf_op jit(solution)/shard_map/all_gather | solution.py:54
  551.5 137.9 %all-reduce.2.cloned.1.call-done = bf16[1792,2048]{0,1:T(8,128)(2,1)} async-done(((bf16[1792,2048]{0,1:T(8,128)(2,1)}), bf16[1792,2048]{0,1:T(8,128)(2,1)}) %all-reduce.2.cloned.1.call-update) | async-done | bytes 7340048 | tf_op jit(solution)/shard_map/psum | solution.py:53
  689.3 9.5 %fusion.5 = f32[1792,512]{1,0:T(8,128)} fusion(bf16[1792,2048]{0,1:T(8,128)(2,1)} %all-reduce.2.cloned.1.call-done, bf16[512,2048]{1,0:T(8,128)(2,1)} %all-gather.17.cloned.1.call-done), kind=kOutput, calls=%fused_computation.15 | convolution fusion | flops 3758096384 | bytes 13107200 | tf_op jit(solution)/shard_map/dot_general | solution.py:55
  (1 shorter events, 0.0 us)
Async XLA Ops:
  6.5 33.1 %all-gather.7.cloned.1.call-start = ((), (), s32[]{:S(2)}) async-start(), calls=%async_computation.2 | async-start | bytes 1310720 | tf_op jit(solution)/shard_map/all_gather | solution.py:24
  7.3 56.0 %all-gather.9.cloned.1.call-start = ((), (), s32[]{:S(2)}) async-start(), calls=%async_computation.3 | async-start | bytes 2621440 | tf_op jit(solution)/shard_map/all_gather | solution.py:25
  8.0 86.7 %all-gather.11.cloned.1.call-start = ((), (), s32[]{:S(2)}) async-start(), calls=%async_computation.4 | async-start | bytes 1310720 | tf_op jit(solution)/shard_map/all_gather | solution.py:31
  66.6 99.9 %reduce-scatter.3.cloned.1.call-start = ((), (), s32[]{:S(2)}) async-start(), calls=%async_computation.5 | async-start | bytes 9175040 | tf_op jit(solution)/shard_map/reduce_scatter | solution.py:35
  101.4 119.0 %all-gather.13.cloned.1.call-start = ((), (), s32[]{:S(2)}) async-start(), calls=%async_computation.6 | async-start | bytes 9175040 | tf_op jit(solution)/shard_map/all_gather | solution.py:40
  166.5 201.3 %reduce-scatter.5.cloned.1.call-start = ((), (), s32[]{:S(2)}) async-start(), calls=%async_computation.7 | async-start | bytes 9175040 | tf_op jit(solution)/shard_map/reduce_scatter | solution.py:44
  239.9 265.7 %all-gather.15.cloned.1.call-start = ((), (), s32[]{:S(2)}) async-start(), calls=%async_computation.8 | async-start | bytes 9175040 | tf_op jit(solution)/shard_map/all_gather | solution.py:50
  372.5 179.0 %all-gather.17.cloned.1.call-start = ((), (), s32[]{:S(2)}) async-start(), calls=%async_computation.10 | async-start | bytes 2621440 | tf_op jit(solution)/shard_map/all_gather | solution.py:54
  373.2 316.1 %all-reduce.2.cloned.1.call-start = ((), (), s32[]{:S(2)}) async-start(), calls=%async_computation.9 | async-start | bytes 14680064 | tf_op jit(solution)/shard_map/psum | solution.py:53
Sparse Core Ops, SparseCore 0:
  8.9 30.6 all-gather.6
  41.1 22.0 all-gather.8
  66.7 27.9 all-gather.10
  101.5 64.9 reduce-scatter.2
  168.0 52.3 all-gather.12
  240.1 127.7 reduce-scatter.4
  372.6 132.9 all-gather.14
  507.3 44.1 all-gather.16
  554.0 135.3 all-reduce.1
where the time goes:
time: 706 us; the launch traced here: 705 us
  waiting for transfers between devices  626 us (89%)
  matrix products  58.6 us (8%)
  between operations  13.2 us (2%)
    psum x1, waiting for transfers between devices, shards(): back_rotated = lax.psum(partial_back.astype(jnp.bfloat16), ('dp', 'rep'))  138 us
    all_gather x1, waiting for transfers between devices, shards(): lax.all_gather(damped, 'mp', axis=1, tiled=True)  132 us
    reduce_scatter x1, waiting for transfers between devices, shards(): lax.psum_scatter(partial_eigen.astype(jnp.bfloat16), 'mp', scatter_dimens...  128 us
    reduce_scatter x1, waiting for transfers between devices, shards(): lax.psum_scatter(partial_grad.astype(jnp.bfloat16), ('dp', 'rep'), scatte...  65.1 us
    all_gather x1, waiting for transfers between devices, shards(): lax.all_gather(grad_block, ('dp', 'rep'), axis=1, tiled=True)  53.8 us
    all_gather x1, waiting for transfers between devices, shards(): features = lax.all_gather(activations, 'mp', axis=1, tiled=True)  31.5 us
    all_gather x1, waiting for transfers between devices, shards(): basis_rows = lax.all_gather(basis_act, 'mp', axis=1, tiled=True)  26.3 us
    all_gather x1, waiting for transfers between devices, shards(): lax.all_gather(rotated, 'mp', axis=1, tiled=True)  25.7 us
  transfers between devices with their start and end apart: 9, of which 9 were waited for; matrix products, arithmetic and copies ran while one was open for 3% of the time, Pallas kernels for 0%

commit v1 on v0

v1 whole, which is shorter than its diff:
```python
import functools

import jax
import jax.numpy as jnp
from jax import lax
from jax.experimental import pallas as pl
from jax.experimental.pallas import tpu as pltpu
from jax.sharding import PartitionSpec as P

LEN = 32
DAMPING = 0.25
STEPS = 16
MESH = pl.DeviceIdType.MESH
VMEM_LIMIT = 60 * 1024 * 1024


def remote(src, dst, send, recv, where):
    return pltpu.make_async_remote_copy(
        src_ref=src, dst_ref=dst, send_sem=send, recv_sem=recv, device_id=where, device_id_type=MESH
    )


def when(there, act):
    if there is True:
        act()
    else:
        pl.when(there)(act)


def z_links(n_mp):
    z = lax.axis_index("mp")
    return [(z > 0, {"mp": z - 1}), (z < n_mp - 1, {"mp": z + 1})]


def x_links(n_dp):
    x = lax.axis_index("dp")
    return [(True, {"dp": lax.rem(x + i, n_dp)}) for i in range(1, n_dp)]


def core_links(n_rep):
    c = lax.axis_index("rep")
    return [(True, {"rep": lax.rem(c + i, n_rep)}) for i in range(1, n_rep)]


def greet(links):
    barrier = pltpu.get_barrier_semaphore()
    for there, where in links:
        when(there, lambda where=where: pl.semaphore_signal(
            barrier, inc=1, device_id=where, device_id_type=MESH))
    pl.semaphore_wait(barrier, sum(1 if there is True else there.astype(jnp.int32) for there, _ in links))


class PlaneGather:
    def __init__(self, src, buf, send, recv, n_dp, n_rep):
        self.src, self.buf, self.send, self.recv = src, buf, send, recv
        self.n_dp, self.n_rep = n_dp, n_rep
        self.rows = src.shape[0]
        self.x, self.c = lax.axis_index("dp"), lax.axis_index("rep")
        self.k = self.x * n_rep + self.c

    def slot(self, k):
        return self.buf.at[pl.ds(pl.multiple_of(k * self.rows, self.rows), self.rows)]

    def first(self):
        out = []
        for n, where in enumerate(w for _, w in x_links(self.n_dp) + core_links(self.n_rep)):
            out.append(remote(self.src, self.slot(self.k), self.send.at[n], self.recv.at[self.k], where))
        return out

    def second(self):
        out = []
        n = self.n_dp + self.n_rep - 2
        for i in range(1, self.n_dp):
            k = lax.rem(self.x + i, self.n_dp) * self.n_rep + self.c
            group = []
            for _, where in core_links(self.n_rep):
                group.append(remote(self.slot(k), self.slot(k), self.send.at[n], self.recv.at[k], where))
                n += 1
            out.append((k, group))
        return out

    def arrive(self, k):
        remote(self.slot(k), self.slot(k), self.send.at[0], self.recv.at[k], {"rep": self.c}).wait_recv()

    def start(self):
        for copy in self.first():
            copy.start()

    def forward(self):
        for k, group in self.second():
            self.arrive(k)
            for copy in group:
                copy.start()

    def finish(self):
        for i in range(self.n_dp):
            for j in range(1, self.n_rep):
                self.arrive(lax.rem(self.x + i, self.n_dp) * self.n_rep + lax.rem(self.c + j, self.n_rep))
        self.slot(self.k)[...] = self.src[...]
        for copy in self.first():
            copy.wait_send()
        for _, group in self.second():
            for copy in group:
                copy.wait_send()


class LineGather:
    def __init__(self, buf, parts, send, recv, n_mp):
        self.buf, self.parts, self.send, self.recv, self.n_mp = buf, parts, send, recv, n_mp
        self.z = lax.axis_index("mp")

    def copy(self, m, h, way):
        i = m * self.parts + h
        return remote(self.buf.at[i], self.buf.at[i], self.send.at[way, i], self.recv.at[i],
                      {"mp": self.z + 2 * way - 1})

    def out(self, m, h, way, act):
        last = self.z < self.n_mp - 1 if way else self.z > 0

        @pl.when(last)
        def _():
            act(self.copy(m, h, way))

    def start(self):
        for h in range(self.parts):
            for way in (0, 1):
                self.out(self.z, h, way, lambda copy: copy.start())

    def take_left(self, m, h):
        self.copy(m, h, 1).wait_recv()
        self.out(m, h, 1, lambda copy: copy.start())

    def take_right(self, m, h):
        self.copy(m, h, 0).wait_recv()
        self.out(m, h, 0, lambda copy: copy.start())

    def step(self, s):
        for h in range(self.parts):
            @pl.when(self.z - s >= 0)
            def _():
                self.take_left(self.z - s, h)

            @pl.when(self.z + s < self.n_mp)
            def _():
                self.take_right(self.z + s, h)

    def finish(self):
        @pl.loop(0, self.n_mp)
        def _(m):
            for h in range(self.parts):
                @pl.when(m <= self.z)
                def _():
                    self.out(m, h, 1, lambda copy: copy.wait_send())

                @pl.when(m >= self.z)
                def _():
                    self.out(m, h, 0, lambda copy: copy.wait_send())


def gather_kernel(n_mp, n_dp, n_rep, fails, ids, s_ref, a_ref, q_ref, s_out, r_out, q_out,
                  s_all, a_all, q_rows, q_cols, r_own, r_all,
                  s_send, s_recv, a_send, a_recv, qr_send, qr_recv, qc_send, qc_recv, r_send, r_recv):
    z = lax.axis_index("mp")
    greet(z_links(n_mp) + x_links(n_dp) + core_links(n_rep))
    s = PlaneGather(s_ref, s_all, s_send, s_recv, n_dp, n_rep)
    qc = PlaneGather(q_ref, q_cols, qc_send, qc_recv, n_dp, n_rep)
    r = PlaneGather(r_own, r_all, r_send, r_recv, n_dp, n_rep)
    a = LineGather(a_all, 1, a_send, a_recv, n_mp)
    qr = LineGather(q_rows, 1, qr_send, qr_recv, n_mp)
    s.start()
    a_all[z] = a_ref[...]
    a.start()
    qc.start()
    q_rows[z] = q_ref[...]
    qr.start()
    for i in range(1, n_mp):
        a.step(i)
    s.forward()
    qc.forward()
    qc.finish()
    depth = a_ref.shape[1]

    total = jnp.zeros((a_ref.shape[0], q_ref.shape[1]), jnp.float32)
    total = lax.fori_loop(
        0, n_mp,
        lambda m, t: t + jnp.dot(a_all[m], q_cols[pl.ds(pl.multiple_of(m * depth, depth), depth), :],
                                 preferred_element_type=jnp.float32),
        total)
    r_own[...] = total.astype(jnp.bfloat16).reshape(r_own.shape)
    r.start()
    s.finish()

    @pl.loop(0, fails)
    def _(i):
        s_out[i] = s_all[ids[i]]

    r.forward()
    r.finish()

    @pl.loop(0, fails)
    def _(i):
        r_out[i] = r_all[ids[i]]

    for i in range(1, n_mp):
        qr.step(i)
    width = q_ref.shape[1]

    @pl.loop(0, n_mp)
    def _(m):
        q_out[:, pl.ds(pl.multiple_of(m * width, width), width)] = q_rows[m]

    a.finish()
    qr.finish()


def sum_kernel(n_mp, u_ref, out_ref, left, right, l_send, l_recv, r_send, r_recv):
    z = lax.axis_index("mp")
    greet(z_links(n_mp))
    rows = u_ref.shape[0] // STEPS

    def at(i):
        return pl.ds(pl.multiple_of(i * rows, rows), rows)

    def copy(buf, i, send, recv, way):
        return remote(buf.at[at(i)], buf.at[at(i)], send.at[i], recv.at[i], {"mp": z + way})

    def take(buf, i, send, recv, way, first, last):
        @pl.when(first)
        def _():
            buf[at(i), :] = u_ref[at(i), :]

        @pl.when(jnp.logical_not(first))
        def _():
            copy(buf, i, send, recv, way).wait_recv()
            buf[at(i), :] = (buf[at(i), :].astype(jnp.float32)
                             + u_ref[at(i), :].astype(jnp.float32)).astype(jnp.bfloat16)

        @pl.when(jnp.logical_not(last))
        def _():
            copy(buf, i, send, recv, way).start()

    @pl.loop(0, STEPS + n_mp - 1)
    def _(t):
        i = t - z
        j = t - (n_mp - 1 - z)

        @pl.when((i >= 0) & (i < STEPS))
        def _():
            take(left, i, l_send, l_recv, 1, z == 0, z == n_mp - 1)

        @pl.when((j >= 0) & (j < STEPS))
        def _():
            take(right, j, r_send, r_recv, -1, z == n_mp - 1, z == 0)

    @pl.loop(0, STEPS)
    def _(i):
        out_ref[at(i), :] = (left[at(i), :].astype(jnp.float32) + right[at(i), :].astype(jnp.float32)
                             - u_ref[at(i), :].astype(jnp.float32)).astype(jnp.bfloat16)

        @pl.when(z < n_mp - 1)
        def _():
            copy(left, i, l_send, l_recv, 1).wait_send()

        @pl.when(z > 0)
        def _():
            copy(right, i, r_send, r_recv, -1).wait_send()


def back_kernel(n_mp, n_dp, n_rep, parts, d_ref, g_ref, out_ref, held, part, other, across,
                z_send, z_recv, c_send, c_recv, x_send, x_recv, o_send, o_recv):
    z, x, c = lax.axis_index("mp"), lax.axis_index("dp"), lax.axis_index("rep")
    greet(z_links(n_mp) + x_links(n_dp) + core_links(n_rep))
    n = n_mp * parts
    rows, width = held.shape[1], held.shape[2]
    half = rows // n_rep
    tile = next(t for t in (256, 128, 64, 32, 16) if rows % t == 0)
    small = next(t for t in (128, 64, 32, 16) if half % t == 0)
    core = {"rep": 1 - c}
    mine = pl.ds(pl.multiple_of(c * half, half), half)
    theirs = pl.ds(pl.multiple_of((1 - c) * half, half), half)
    line = LineGather(held, parts, z_send, z_recv, n_mp)

    for h in range(parts):
        held[z * parts + h] = d_ref[:, h * width:(h + 1) * width]
    line.start()

    low, high = z, n_mp - 1 - z
    near = jnp.minimum(low, high)
    both = 2 * near * parts

    def place(p):
        q = p - parts
        pair, turn = q // (2 * parts), q % (2 * parts)
        far = q - both
        is_pair = q < both
        s = jnp.where(is_pair, pair + 1, near + far // parts + 1)
        h = jnp.where(is_pair, turn // 2, far % parts)
        from_left = jnp.where(is_pair, turn % 2 == 0, low > high)
        own = p < parts
        m = jnp.where(own, z, jnp.where(from_left, z - s, z + s))
        return m, jnp.where(own, p, h), own, from_left

    def columns(p):
        m, h, _, _ = place(p)
        return pl.ds(pl.multiple_of((m * parts + h) * width, width), width)

    def core_copy(p):
        return remote(part.at[p, theirs], other.at[p], c_send.at[p], c_recv.at[p], core)

    def x_copies(p):
        return [remote(part.at[p, mine], across.at[p, i - 1], x_send.at[p, i - 1], x_recv.at[p, i - 1],
                       {"dp": lax.rem(x + i, n_dp)}) for i in range(1, n_dp)]

    def out_copy(p, whose):
        return remote(out_ref.at[whose, columns(p)], out_ref.at[whose, columns(p)], o_send.at[p], o_recv.at[p], core)

    def multiply(p):
        m, h, own, from_left = place(p)

        @pl.when(jnp.logical_not(own) & from_left)
        def _():
            line.take_left(m, h)

        @pl.when(jnp.logical_not(own) & jnp.logical_not(from_left))
        def _():
            line.take_right(m, h)

        @pl.loop(0, rows // tile)
        def _(t):
            at = pl.ds(pl.multiple_of(t * tile, tile), tile)
            part[p, at, :] = jnp.dot(
                g_ref[at, :], held[m * parts + h], preferred_element_type=jnp.float32).astype(jnp.bfloat16)

        core_copy(p).start()

    def add_cores(p):
        core_copy(p).wait()

        @pl.loop(0, half // small)
        def _(t):
            here = pl.ds(pl.multiple_of(c * half + t * small, small), small)
            at = pl.ds(pl.multiple_of(t * small, small), small)
            part[p, here, :] = (part[p, here, :].astype(jnp.float32)
                                + other[p, at, :].astype(jnp.float32)).astype(jnp.bfloat16)

        for copy in x_copies(p):
            copy.start()

    def add_chips(p):
        for copy in x_copies(p):
            copy.wait()

        @pl.loop(0, half // small)
        def _(t):
            here = pl.ds(pl.multiple_of(c * half + t * small, small), small)
            at = pl.ds(pl.multiple_of(t * small, small), small)
            total = part[p, here, :].astype(jnp.float32)
            for i in range(n_dp - 1):
                total += across[p, i, at, :].astype(jnp.float32)
            out_ref[here, columns(p)] = total.astype(jnp.bfloat16)

        out_copy(p, mine).start()

    @pl.loop(0, n + 2)
    def _(t):
        @pl.when(t < n)
        def _():
            multiply(t)

        @pl.when((t >= 1) & (t < n + 1))
        def _():
            add_cores(t - 1)

        @pl.when(t >= 2)
        def _():
            add_chips(t - 2)

    @pl.loop(0, n)
    def _(p):
        out_copy(p, mine).wait_send()
        out_copy(p, theirs).wait_recv()

    line.finish()


def shards(n_mp, n_dp, n_rep, activations, out_grads, basis_grad, basis_act, eigen_values, token_counts, fail_ids):
    tokens, features = activations.shape
    hidden = out_grads.shape[1]
    wide = basis_grad.shape[1]
    rows = basis_act.shape[0]
    planes = n_dp * n_rep
    fails = fail_ids.shape[0]
    prompts = token_counts.shape[0]
    live = fails * LEN
    bf16 = jnp.bfloat16
    dma = pltpu.SemaphoreType.DMA
    vmem = pl.BlockSpec(memory_space=pltpu.VMEM)
    live_slot = jnp.arange(LEN, dtype=jnp.int32)[None, :] < token_counts[:, None]
    inverse = 1.0 / token_counts.astype(jnp.float32)
    weight = jnp.where(live_slot, inverse[:, None], jnp.float32(0.0)).reshape(tokens)
    scaled = (out_grads.astype(jnp.float32) * weight[:, None]).astype(bf16)

    sends = n_dp + n_rep - 2 + (n_dp - 1) * (n_rep - 1)
    plane_sems = [dma((sends,)), dma((planes,))]
    line_sems = [dma((2, n_mp)), dma((n_mp,))]
    grads, rotated, basis_rows = pl.pallas_call(
        functools.partial(gather_kernel, n_mp, n_dp, n_rep, fails),
        out_shape=(
            jax.ShapeDtypeStruct((fails, LEN, hidden), bf16),
            jax.ShapeDtypeStruct((fails, LEN, features), bf16),
            jax.ShapeDtypeStruct((rows, n_mp * features), bf16),
        ),
        in_specs=[pl.BlockSpec(memory_space=pltpu.SMEM), vmem, vmem, vmem],
        out_specs=(vmem, vmem, vmem),
        scratch_shapes=[
            pltpu.VMEM((planes * prompts, LEN, hidden), bf16),
            pltpu.VMEM((n_mp, tokens, features), bf16),
            pltpu.VMEM((n_mp, rows, features), bf16),
            pltpu.VMEM((planes * rows, features), bf16),
            pltpu.VMEM((prompts, LEN, features), bf16),
            pltpu.VMEM((planes * prompts, LEN, features), bf16),
        ] + plane_sems + line_sems + line_sems + plane_sems + plane_sems,
        compiler_params=pltpu.CompilerParams(
            collective_id=0, has_side_effects=True, vmem_limit_bytes=VMEM_LIMIT),
        name="gather_inputs",
    )(fail_ids, scaled.reshape(prompts, LEN, hidden), activations, basis_act)

    grads, rotated = grads.reshape(live, hidden), rotated.reshape(live, features)
    partial_u = jnp.dot(grads, basis_grad, preferred_element_type=jnp.float32).astype(bf16)
    turned = pl.pallas_call(
        functools.partial(sum_kernel, n_mp),
        out_shape=jax.ShapeDtypeStruct((live, wide), bf16),
        in_specs=[vmem],
        out_specs=vmem,
        scratch_shapes=[
            pltpu.VMEM((live, wide), bf16),
            pltpu.VMEM((live, wide), bf16),
        ] + [dma((STEPS,))] * 4,
        compiler_params=pltpu.CompilerParams(
            collective_id=1, has_side_effects=True, vmem_limit_bytes=VMEM_LIMIT),
        name="sum_turned",
    )(partial_u)

    eigen_grad = lax.dot_general(
        turned, rotated, (((0,), (0,)), ((), ())), preferred_element_type=jnp.float32)
    damped = (eigen_grad / (eigen_values + DAMPING)).astype(bf16)

    parts = max(1, features // 256)
    width = features // parts
    n = n_mp * parts
    half = hidden // n_rep
    back = pl.pallas_call(
        functools.partial(back_kernel, n_mp, n_dp, n_rep, parts),
        out_shape=jax.ShapeDtypeStruct((hidden, n_mp * features), bf16),
        in_specs=[vmem, vmem],
        out_specs=vmem,
        scratch_shapes=[
            pltpu.VMEM((n, wide, width), bf16),
            pltpu.VMEM((n, hidden, width), bf16),
            pltpu.VMEM((n, half, width), bf16),
            pltpu.VMEM((n, n_dp - 1, half, width), bf16),
            dma((2, n)), dma((n,)),
            dma((n,)), dma((n,)),
            dma((n, n_dp - 1)), dma((n, n_dp - 1)),
            dma((n,)), dma((n,)),
        ],
        compiler_params=pltpu.CompilerParams(
            collective_id=2, has_side_effects=True, vmem_limit_bytes=VMEM_LIMIT),
        name="back_rotate",
    )(damped, basis_grad)
    return lax.dot_general(
        back, basis_rows, (((1,), (1,)), ((), ())), preferred_element_type=jnp.float32)


def solution(mesh):
    return jax.shard_map(
        functools.partial(shards, mesh.shape["mp"], mesh.shape["dp"], mesh.shape["rep"]),
        mesh=mesh,
        in_specs=(
            P(("groups", "dp", "rep"), "mp"),
            P(("groups", "dp", "rep"), "mp"),
            P(("groups", "mp"), ("dp", "rep")),
            P(("groups", "dp", "rep"), "mp"),
            P(("groups", "dp", "rep"), "mp"),
            P(("groups", "dp", "rep")),
            P("groups"),
        ),
        out_specs=P(("groups", "mp"), ("dp", "rep")),
        check_vma=False,
    )
```

time: 706 us -> 346 us (0.49)
  waiting for transfers between devices: 626 us -> 0 us
  Pallas kernels: 0 us -> 318 us
  matrix products: 58.6 us -> 23.5 us
  between operations: 13.2 us -> 0.04 us
    pallas_call x0 -> x3, Pallas kernels: none -> 318 us  [the longest x1 148 us: shards(): pl.pallas_call(functools.partial(back_kernel, n_mp, n_dp, n_rep, parts),...]
    all_gather x6 -> x0, waiting for transfers between devices: 293 us -> none  [the longest x1 132 us: shards(): lax.all_gather(damped, 'mp', axis=1, tiled=True)]
    reduce_scatter x2 -> x0, waiting for transfers between devices: 193 us -> none  [the longest x1 128 us: shards(): lax.psum_scatter(partial_eigen.astype(jnp.bfloat16), 'mp', scatter_dimens...]
    psum x1 -> x0, waiting for transfers between devices: 138 us -> none  [shards(): back_rotated = lax.psum(partial_back.astype(jnp.bfloat16), ('dp', 'rep'))]
    dot_general x5 -> x3, matrix products: 58.6 us -> 23.5 us  [the longest x1 9.67 us: shards(): jnp.dot(grads, basis_grad, preferred_element_type=jnp.float32).astype(bf16)]
  transfers between devices with their start and end apart: 9 -> 0, of which waited for: 9 -> 0; matrix products, arithmetic and copies ran while one was open for 3% -> 0% of each run, Pallas kernels for 0% -> 0%
where the time goes in v1:
time: 346 us
  Pallas kernels  318 us (92%)
  matrix products  23.5 us (7%)
  other arithmetic  3.71 us (1%)
    pallas_call x1, Pallas kernels, shards(): pl.pallas_call(functools.partial(back_kernel, n_mp, n_dp, n_rep, parts),...  148 us
    pallas_call x1, Pallas kernels, shards(): pl.pallas_call(functools.partial(sum_kernel, n_mp), out_shape=jax.ShapeDt...  91 us
    pallas_call x1, Pallas kernels, shards(): pl.pallas_call(functools.partial(gather_kernel, n_mp, n_dp, n_rep, fails)...  79.6 us
    dot_general x1, matrix products, shards(): jnp.dot(grads, basis_grad, preferred_element_type=jnp.float32).astype(bf16)  9.67 us
    dot_general x1, matrix products, shards(): lax.dot_general(back, basis_rows, (((1,), (1,)), ((), ())), preferred_ele...  8.94 us

profile of v1, /device:TPU:0, one launch (start us, length us, event | category | flops | bytes accessed | tf_op | source)
XLA Modules:
  0.0 345.5 jit_solution(6497010322223428157)
XLA Ops:
  0.0 0.7 convert_divide_fusion
  0.7 0.7 fusion
  1.4 0.1 select_n.12
  1.5 2.3 multiply_convert_fusion
  3.8 79.6 %gather_inputs.1 = (bf16[24,32,1792]{2,1,0:T(8,128)(2,1)}, bf16[24,32,512]{2,1,0:T(8,128)(2,1)}, bf16[512,2048]{1,0:T(8,128)(2,1)}) custom-call(s32[24]{0:T(128)} %ids.1, bf16[8,32,1792]{2,1,0:T(8,128)(2,1)} %bitcast.9, bf16[256,512]{1,0:T(8,128)(2,1)} %a_ref.1, bf16[512,512]{1,0:T(8,128)(2,1)} %q_ref.1), custom_call_target="tpu_custom_call" | custom-call | tf_op jit(solution)/shard_map/gather_inputs/pallas_call | solution.py:406
  83.4 9.7 %convolution_convert_fusion.u_ref = bf16[768,1792]{1,0:T(8,128)(2,1)} fusion(bf16[768,1792]{1,0:T(8,128)(2,1)} %bitcast.10, bf16[1792,1792]{1,0:T(8,128)(2,1)} %g_ref.1), kind=kOutput, calls=%fused_computation.1 | convolution fusion | flops 4933877760 | bytes 11927552 | tf_op jit(solution)/shard_map/dot_general | solution.py:429
  93.1 0.0 copy-start
  93.1 91.0 %sum_turned.1 = bf16[768,1792]{1,0:T(8,128)(2,1)} custom-call(bf16[768,1792]{1,0:T(8,128)(2,1)} %convolution_convert_fusion.u_ref), custom_call_target="tpu_custom_call" | custom-call | tf_op jit(solution)/shard_map/sum_turned/pallas_call | solution.py:430
  184.1 0.0 copy-done
  184.1 4.9 %divide_convert_fusion.d_ref = bf16[1792,512]{1,0:T(8,128)(2,1)} fusion(f32[1792,512]{1,0:T(8,128)S(1)} %copy-done, bf16[768,1792]{1,0:T(8,128)(2,1)} %sum_turned.1, bf16[768,512]{1,0:T(8,128)(2,1)} %bitcast.11), kind=kOutput, calls=%fused_computation | convolution fusion | flops 1412038656 | bytes 9043968 | tf_op jit(solution)/shard_map/dot_general | solution.py:444
  189.0 0.0 copy-start.1
  189.0 147.5 %back_rotate.1 = bf16[1792,2048]{1,0:T(8,128)(2,1)} custom-call(bf16[1792,512]{1,0:T(8,128)(2,1)} %divide_convert_fusion.d_ref, bf16[1792,1792]{1,0:T(8,128)(2,1)} %g_ref.1), custom_call_target="tpu_custom_call" | custom-call | tf_op jit(solution)/shard_map/back_rotate/pallas_call | solution.py:452
  336.6 0.0 copy-done.1
  336.6 8.9 %fusion.1 = f32[1792,512]{1,0:T(8,128)} fusion(bf16[1792,2048]{1,0:T(8,128)(2,1)} %back_rotate.1, bf16[512,2048]{1,0:T(8,128)(2,1)S(1)} %copy-done.1), kind=kOutput, calls=%fused_computation.6 | convolution fusion | flops 3758096384 | bytes 13107200 | tf_op jit(solution)/shard_map/dot_general | solution.py:471
Async XLA Ops:
  93.1 91.0 %copy-start = (f32[1792,512]{1,0:T(8,128)S(1)}, f32[1792,512]{1,0:T(8,128)}, u32[]{:S(2)}) copy-start(f32[1792,512]{1,0:T(8,128)} %param.11) | copy-start | bytes 11010052
  189.0 147.6 %copy-start.1 = (bf16[512,2048]{1,0:T(8,128)(2,1)S(1)}, bf16[512,2048]{1,0:T(8,128)(2,1)}, u32[]{:S(2)}) copy-start(bf16[512,2048]{1,0:T(8,128)(2,1)} %get-tuple-element.10) | copy-start | bytes 6291460

commit v2 on v1

--- a/solution.py
+++ b/solution.py
@@ -157,54 +157,146 @@
                     self.out(m, h, 0, lambda copy: copy.wait_send())
 
 
-def gather_kernel(n_mp, n_dp, n_rep, fails, ids, s_ref, a_ref, q_ref, s_out, r_out, q_out,
-                  s_all, a_all, q_rows, q_cols, r_own, r_all,
-                  s_send, s_recv, a_send, a_recv, qr_send, qr_recv, qc_send, qc_recv, r_send, r_recv):
+def turn_kernel(n_mp, n_dp, n_rep, fails, ids, counts, g_ref, a_ref, q_ref, basis_ref, u_out, r_out, q_out,
+                s_own, s_all, s_block, a_all, q_rows, q_cols, r_own, r_all, u_own, left, right,
+                s_send, s_recv, a_send, a_recv, qr_send, qr_recv, qc_send, qc_recv, r_send, r_recv,
+                ul_send, ul_recv, ur_send, ur_recv):
     z = lax.axis_index("mp")
     greet(z_links(n_mp) + x_links(n_dp) + core_links(n_rep))
-    s = PlaneGather(s_ref, s_all, s_send, s_recv, n_dp, n_rep)
+    s = PlaneGather(s_own, s_all, s_send, s_recv, n_dp, n_rep)
     qc = PlaneGather(q_ref, q_cols, qc_send, qc_recv, n_dp, n_rep)
     r = PlaneGather(r_own, r_all, r_send, r_recv, n_dp, n_rep)
     a = LineGather(a_all, 1, a_send, a_recv, n_mp)
     qr = LineGather(q_rows, 1, qr_send, qr_recv, n_mp)
-    s.start()
+    depth, width = a_ref.shape[1], q_ref.shape[1]
+    wide = basis_ref.shape[1]
+    rows = u_own.shape[0] // STEPS
+    blocks = u_own.shape[0] // (s_block.shape[0] * LEN)
+    per = STEPS // blocks
+    tile = 256 if wide % 256 == 0 else wide
+
     a_all[z] = a_ref[...]
     a.start()
-    qc.start()
+
+    @pl.loop(0, counts.shape[0])
+    def _(i):
+        count = jnp.full((LEN, 1), counts[i], jnp.int32)
+        slot = lax.broadcasted_iota(jnp.int32, (LEN, 1), 0)
+        weight = jnp.where(slot < count, 1.0 / count.astype(jnp.float32), 0.0)
+        s_own[i] = (g_ref[i].astype(jnp.float32) * weight).astype(jnp.bfloat16)
+
+    s.start()
     q_rows[z] = q_ref[...]
+    a.step(1)
     qr.start()
-    for i in range(1, n_mp):
+    for i in range(2, n_mp):
         a.step(i)
     s.forward()
-    qc.forward()
-    qc.finish()
-    depth = a_ref.shape[1]
-
-    total = jnp.zeros((a_ref.shape[0], q_ref.shape[1]), jnp.float32)
-    total = lax.fori_loop(
-        0, n_mp,
-        lambda m, t: t + jnp.dot(a_all[m], q_cols[pl.ds(pl.multiple_of(m * depth, depth), depth), :],
-                                 preferred_element_type=jnp.float32),
-        total)
-    r_own[...] = total.astype(jnp.bfloat16).reshape(r_own.shape)
-    r.start()
+    qc.start()
     s.finish()
 
-    @pl.loop(0, fails)
+    def at(i):
+        return pl.ds(pl.multiple_of(i * rows, rows), rows)
+
+    def copy(buf, i, send, recv, way):
+        return remote(buf.at[at(i)], buf.at[at(i)], send.at[i], recv.at[i], {"mp": z + way})
+
+    def take(buf, i, send, recv, way, first, last):
+        @pl.when(first)
+        def _():
+            buf[at(i), :] = u_own[at(i), :]
+
+        @pl.when(jnp.logical_not(first))
+        def _():
+            copy(buf, i, send, recv, way).wait_recv()
+            buf[at(i), :] = (buf[at(i), :].astype(jnp.float32)
+                             + u_own[at(i), :].astype(jnp.float32)).astype(jnp.bfloat16)
+
+        @pl.when(jnp.logical_not(last))
+        def _():
+            copy(buf, i, send, recv, way).start()
+
+    def turn(block):
+        prompts = s_block.shape[0]
+
+        @pl.loop(0, prompts)
+        def _(i):
+            s_block[i] = s_all[ids[block * prompts + i]]
+
+        size = prompts * LEN
+        here = pl.ds(pl.multiple_of(block * size, size), size)
+
+        @pl.loop(0, wide // tile)
+        def _(j):
+            cols = pl.ds(pl.multiple_of(j * tile, tile), tile)
+            u_own[here, cols] = jnp.dot(
+                s_block[...].reshape(size, s_block.shape[2]), basis_ref[:, cols],
+                preferred_element_type=jnp.float32).astype(jnp.bfloat16)
+
+    def rotate():
+        qc.finish()
+        total = jnp.zeros((a_ref.shape[0], width), jnp.float32)
+        total = lax.fori_loop(
+            0, n_mp,
+            lambda m, t: t + jnp.dot(a_all[m], q_cols[pl.ds(pl.multiple_of(m * depth, depth), depth), :],
+                                     preferred_element_type=jnp.float32),
+            total)
+        r_own[...] = total.astype(jnp.bfloat16).reshape(r_own.shape)
+        r.start()
+
+    @pl.loop(0, STEPS + n_mp - 1)
+    def _(t):
+        @pl.when((t < STEPS) & (t % per == 0))
+        def _():
+            turn(t // per)
+
+        i = t - z
+        j = t - (n_mp - 1 - z)
+
+        @pl.when((i >= 0) & (i < STEPS))
+        def _():
+            take(left, i, ul_send, ul_recv, 1, z == 0, z == n_mp - 1)
+
+        @pl.when((j >= 0) & (j < STEPS))
+        def _():
+            take(right, j, ur_send, ur_recv, -1, z == n_mp - 1, z == 0)
+
+        for n in range(1, n_mp):
+            @pl.when(t == (n - 1) * STEPS // (n_mp - 1))
+            def _():
+                qr.step(n)
+
+        @pl.when(t == STEPS // 2)
+        def _():
+            qc.forward()
+
+        @pl.when(t == 3 * STEPS // 4)
+        def _():
+            rotate()
+
+        @pl.when(t == STEPS)
+        def _():
+            r.forward()
+
+    @pl.loop(0, STEPS)
     def _(i):
-        s_out[i] = s_all[ids[i]]
-
-    r.forward()
+        u_out[at(i), :] = (left[at(i), :].astype(jnp.float32) + right[at(i), :].astype(jnp.float32)
+                           - u_own[at(i), :].astype(jnp.float32)).astype(jnp.bfloat16)
+
+        @pl.when(z < n_mp - 1)
+        def _():
+            copy(left, i, ul_send, ul_recv, 1).wait_send()
+
+        @pl.when(z > 0)
+        def _():
+            copy(right, i, ur_send, ur_recv, -1).wait_send()
+
     r.finish()
 
     @pl.loop(0, fails)
     def _(i):
         r_out[i] = r_all[ids[i]]
 
-    for i in range(1, n_mp):
-        qr.step(i)
-    width = q_ref.shape[1]
-
     @pl.loop(0, n_mp)
     def _(m):
         q_out[:, pl.ds(pl.multiple_of(m * width, width), width)] = q_rows[m]
@@ -213,60 +305,7 @@
     qr.finish()
 
 
-def sum_kernel(n_mp, u_ref, out_ref, left, right, l_send, l_recv, r_send, r_recv):
-    z = lax.axis_index("mp")
-    greet(z_links(n_mp))
-    rows = u_ref.shape[0] // STEPS
-
-    def at(i):
-        return pl.ds(pl.multiple_of(i * rows, rows), rows)
-
-    def copy(buf, i, send, recv, way):
-        return remote(buf.at[at(i)], buf.at[at(i)], send.at[i], recv.at[i], {"mp": z + way})
-
-    def take(buf, i, send, recv, way, first, last):
-        @pl.when(first)
-        def _():
-            buf[at(i), :] = u_ref[at(i), :]
-
-        @pl.when(jnp.logical_not(first))
-        def _():
-            copy(buf, i, send, recv, way).wait_recv()
-            buf[at(i), :] = (buf[at(i), :].astype(jnp.float32)
-                             + u_ref[at(i), :].astype(jnp.float32)).astype(jnp.bfloat16)
-
-        @pl.when(jnp.logical_not(last))
-        def _():
-            copy(buf, i, send, recv, way).start()
-
-    @pl.loop(0, STEPS + n_mp - 1)
-    def _(t):
-        i = t - z
-        j = t - (n_mp - 1 - z)
-
-        @pl.when((i >= 0) & (i < STEPS))
-        def _():
-            take(left, i, l_send, l_recv, 1, z == 0, z == n_mp - 1)
-
-        @pl.when((j >= 0) & (j < STEPS))
-        def _():
-            take(right, j, r_send, r_recv, -1, z == n_mp - 1, z == 0)
-
-    @pl.loop(0, STEPS)
-    def _(i):
-        out_ref[at(i), :] = (left[at(i), :].astype(jnp.float32) + right[at(i), :].astype(jnp.float32)
-                             - u_ref[at(i), :].astype(jnp.float32)).astype(jnp.bfloat16)
-
-        @pl.when(z < n_mp - 1)
-        def _():
-            copy(left, i, l_send, l_recv, 1).wait_send()
-
-        @pl.when(z > 0)
-        def _():
-            copy(right, i, r_send, r_recv, -1).wait_send()
-
-
-def back_kernel(n_mp, n_dp, n_rep, parts, d_ref, g_ref, out_ref, held, part, other, across,
+def back_kernel(n_mp, n_dp, n_rep, parts, d_ref, g_ref, q_ref, out_ref, back, held, part, other, across,
                 z_send, z_recv, c_send, c_recv, x_send, x_recv, o_send, o_recv):
     z, x, c = lax.axis_index("mp"), lax.axis_index("dp"), lax.axis_index("rep")
     greet(z_links(n_mp) + x_links(n_dp) + core_links(n_rep))
@@ -312,7 +351,7 @@
                        {"dp": lax.rem(x + i, n_dp)}) for i in range(1, n_dp)]
 
     def out_copy(p, whose):
-        return remote(out_ref.at[whose, columns(p)], out_ref.at[whose, columns(p)], o_send.at[p], o_recv.at[p], core)
+        return remote(back.at[whose, columns(p)], back.at[whose, columns(p)], o_send.at[p], o_recv.at[p], core)
 
     def multiply(p):
         m, h, own, from_left = place(p)
@@ -357,11 +396,23 @@
             total = part[p, here, :].astype(jnp.float32)
             for i in range(n_dp - 1):
                 total += across[p, i, at, :].astype(jnp.float32)
-            out_ref[here, columns(p)] = total.astype(jnp.bfloat16)
+            back[here, columns(p)] = total.astype(jnp.bfloat16)
 
         out_copy(p, mine).start()
 
-    @pl.loop(0, n + 2)
+    def finish(p):
+        out_copy(p, theirs).wait_recv()
+        cols = columns(p)
+
+        @pl.loop(0, rows // tile)
+        def _(t):
+            at = pl.ds(pl.multiple_of(t * tile, tile), tile)
+            out_ref[at, :] += lax.dot_general(
+                back[at, cols], q_ref[:, cols], (((1,), (1,)), ((), ())), preferred_element_type=jnp.float32)
+
+    out_ref[...] = jnp.zeros_like(out_ref)
+
+    @pl.loop(0, n + 3)
     def _(t):
         @pl.when(t < n)
         def _():
@@ -371,14 +422,17 @@
         def _():
             add_cores(t - 1)
 
-        @pl.when(t >= 2)
+        @pl.when((t >= 2) & (t < n + 2))
         def _():
             add_chips(t - 2)
+
+        @pl.when(t >= 3)
+        def _():
+            finish(t - 3)
 
     @pl.loop(0, n)
     def _(p):
         out_copy(p, mine).wait_send()
-        out_copy(p, theirs).wait_recv()
 
     line.finish()
 
@@ -395,51 +449,38 @@
     bf16 = jnp.bfloat16
     dma = pltpu.SemaphoreType.DMA
     vmem = pl.BlockSpec(memory_space=pltpu.VMEM)
-    live_slot = jnp.arange(LEN, dtype=jnp.int32)[None, :] < token_counts[:, None]
-    inverse = 1.0 / token_counts.astype(jnp.float32)
-    weight = jnp.where(live_slot, inverse[:, None], jnp.float32(0.0)).reshape(tokens)
-    scaled = (out_grads.astype(jnp.float32) * weight[:, None]).astype(bf16)
-
     sends = n_dp + n_rep - 2 + (n_dp - 1) * (n_rep - 1)
     plane_sems = [dma((sends,)), dma((planes,))]
     line_sems = [dma((2, n_mp)), dma((n_mp,))]
-    grads, rotated, basis_rows = pl.pallas_call(
-        functools.partial(gather_kernel, n_mp, n_dp, n_rep, fails),
+    smem = pl.BlockSpec(memory_space=pltpu.SMEM)
+    blocks = next(b for b in (4, 2, 1) if fails % b == 0 and STEPS % b == 0)
+    turned, rotated, basis_rows = pl.pallas_call(
+        functools.partial(turn_kernel, n_mp, n_dp, n_rep, fails),
         out_shape=(
-            jax.ShapeDtypeStruct((fails, LEN, hidden), bf16),
+            jax.ShapeDtypeStruct((live, wide), bf16),
             jax.ShapeDtypeStruct((fails, LEN, features), bf16),
             jax.ShapeDtypeStruct((rows, n_mp * features), bf16),
         ),
-        in_specs=[pl.BlockSpec(memory_space=pltpu.SMEM), vmem, vmem, vmem],
+        in_specs=[smem, smem, vmem, vmem, vmem, vmem],
         out_specs=(vmem, vmem, vmem),
         scratch_shapes=[
+            pltpu.VMEM((prompts, LEN, hidden), bf16),
             pltpu.VMEM((planes * prompts, LEN, hidden), bf16),
+            pltpu.VMEM((fails // blocks, LEN, hidden), bf16),
             pltpu.VMEM((n_mp, tokens, features), bf16),
             pltpu.VMEM((n_mp, rows, features), bf16),
             pltpu.VMEM((planes * rows, features), bf16),
             pltpu.VMEM((prompts, LEN, features), bf16),
             pltpu.VMEM((planes * prompts, LEN, features), bf16),
-        ] + plane_sems + line_sems + line_sems + plane_sems + plane_sems,
+            pltpu.VMEM((live, wide), bf16),
+            pltpu.VMEM((live, wide), bf16),
+            pltpu.VMEM((live, wide), bf16),
+        ] + plane_sems + line_sems + line_sems + plane_sems + plane_sems + [dma((STEPS,))] * 4,
         compiler_params=pltpu.CompilerParams(
             collective_id=0, has_side_effects=True, vmem_limit_bytes=VMEM_LIMIT),
-        name="gather_inputs",
-    )(fail_ids, scaled.reshape(prompts, LEN, hidden), activations, basis_act)
-
-    grads, rotated = grads.reshape(live, hidden), rotated.reshape(live, features)
-    partial_u = jnp.dot(grads, basis_grad, preferred_element_type=jnp.float32).astype(bf16)
-    turned = pl.pallas_call(
-        functools.partial(sum_kernel, n_mp),
-        out_shape=jax.ShapeDtypeStruct((live, wide), bf16),
-        in_specs=[vmem],
-        out_specs=vmem,
-        scratch_shapes=[
-            pltpu.VMEM((live, wide), bf16),
-            pltpu.VMEM((live, wide), bf16),
-        ] + [dma((STEPS,))] * 4,
-        compiler_params=pltpu.CompilerParams(
-            collective_id=1, has_side_effects=True, vmem_limit_bytes=VMEM_LIMIT),
-        name="sum_turned",
-    )(partial_u)
+        name="turn_grads",
+    )(fail_ids, token_counts, out_grads.reshape(prompts, LEN, hidden), activations, basis_act, basis_grad)
+    rotated = rotated.reshape(live, features)
 
     eigen_grad = lax.dot_general(
         turned, rotated, (((0,), (0,)), ((), ())), preferred_element_type=jnp.float32)
@@ -449,12 +490,13 @@
     width = features // parts
     n = n_mp * parts
     half = hidden // n_rep
-    back = pl.pallas_call(
+    return pl.pallas_call(
         functools.partial(back_kernel, n_mp, n_dp, n_rep, parts),
-        out_shape=jax.ShapeDtypeStruct((hidden, n_mp * features), bf16),
-        in_specs=[vmem, vmem],
+        out_shape=jax.ShapeDtypeStruct((hidden, rows), jnp.float32),
+        in_specs=[vmem, vmem, vmem],
         out_specs=vmem,
         scratch_shapes=[
+            pltpu.VMEM((hidden, n_mp * features), bf16),
             pltpu.VMEM((n, wide, width), bf16),
             pltpu.VMEM((n, hidden, width), bf16),
             pltpu.VMEM((n, half, width), bf16),
@@ -465,11 +507,9 @@
             dma((n,)), dma((n,)),
         ],
         compiler_params=pltpu.CompilerParams(
-            collective_id=2, has_side_effects=True, vmem_limit_bytes=VMEM_LIMIT),
+            collective_id=1, has_side_effects=True, vmem_limit_bytes=VMEM_LIMIT),
         name="back_rotate",
-    )(damped, basis_grad)
-    return lax.dot_general(
-        back, basis_rows, (((1,), (1,)), ((), ())), preferred_element_type=jnp.float32)
+    )(damped, basis_grad, basis_rows)
 
 
 def solution(mesh):

time: 346 us -> 306 us (0.88)
  Pallas kernels: 318 us -> 297 us
  matrix products: 23.5 us -> 4.91 us
  local copies, waits for them, and re-layouts: 0.09 us -> 4.25 us
  other arithmetic: 3.71 us -> 0 us
    pallas_call x2 -> x1, Pallas kernels: 171 us -> 148 us  [shards(): pl.pallas_call(functools.partial(turn_kernel, n_mp, n_dp, n_rep, fails),...]
    dot_general x2 -> x0, matrix products: 18.6 us -> none  [the longest x1 9.67 us: shards(): jnp.dot(grads, basis_grad, preferred_element_type=jnp.float32).astype(bf16)]
    unnamed x4 -> x3, local copies, waits for them, and re-layouts: 0.01 us -> 4.25 us
where the time goes in v2:
time: 306 us
  Pallas kernels  297 us (97%)
  matrix products  4.91 us (2%)
  local copies, waits for them, and re-layouts  4.25 us (1%)
    pallas_call x1, Pallas kernels, shards(): pl.pallas_call(functools.partial(back_kernel, n_mp, n_dp, n_rep, parts),...  148 us
    pallas_call x1, Pallas kernels, shards(): pl.pallas_call(functools.partial(turn_kernel, n_mp, n_dp, n_rep, fails),...  148 us

profile of v2, /device:TPU:0, one launch (start us, length us, event | category | flops | bytes accessed | tf_op | source)
XLA Modules:
  0.0 305.7 jit_solution(15302947318503118360)
XLA Ops:
  0.0 0.0 copy-start
  0.0 148.0 %turn_grads.1 = (bf16[768,1792]{1,0:T(8,128)(2,1)}, bf16[24,32,512]{2,1,0:T(8,128)(2,1)}, bf16[512,2048]{1,0:T(8,128)(2,1)}) custom-call(s32[24]{0:T(128)} %ids.1, s32[8]{0:T(128)} %counts.1, bf16[8,32,1792]{2,1,0:T(8,128)(2,1)} %bitcast.4, bf16[256,512]{1,0:T(8,128)(2,1)} %a_ref.1, bf16[512,512]{1,0:T(8,128)(2,1)} %q_ref.1, bf16[1792,1792]{1,0:T(8,128)(2,1)} %g_ref.1), custom_call_target="tpu_custom_call" | custom-call | tf_op jit(solution)/shard_map/turn_grads/pallas_call | solution.py:457
  148.0 0.0 copy-done
  148.1 4.9 %divide_convert_fusion.d_ref = bf16[1792,512]{1,0:T(8,128)(2,1)} fusion(f32[1792,512]{1,0:T(8,128)S(1)} %copy-done, bf16[768,1792]{1,0:T(8,128)(2,1)} %get-tuple-element.8, bf16[768,512]{1,0:T(8,128)(2,1)} %bitcast.5), kind=kOutput, calls=%fused_computation | convolution fusion | flops 1412038656 | bytes 9043968 | tf_op jit(solution)/shard_map/dot_general | solution.py:485
  153.0 148.5 %back_rotate.1 = f32[1792,512]{1,0:T(8,128)} custom-call(bf16[1792,512]{1,0:T(8,128)(2,1)} %divide_convert_fusion.d_ref, bf16[1792,1792]{1,0:T(8,128)(2,1)} %g_ref.1, bf16[512,2048]{1,0:T(8,128)(2,1)} %get-tuple-element.10.q_ref), custom_call_target="tpu_custom_call" | custom-call | tf_op jit(solution)/shard_map/back_rotate/pallas_call | solution.py:493
  301.4 4.2 %copy.9 = f32[1792,512]{1,0:T(8,128)} copy(f32[1792,512]{1,0:T(8,128)} %back_rotate.1) | data formatting | bytes 7340032
Async XLA Ops:
  0.0 148.0 %copy-start = (f32[1792,512]{1,0:T(8,128)S(1)}, f32[1792,512]{1,0:T(8,128)}, u32[]{:S(2)}) copy-start(f32[1792,512]{1,0:T(8,128)} %param.11) | copy-start | bytes 11010052

commit v3 on v2

--- a/solution.py
+++ b/solution.py
@@ -9,7 +9,8 @@
 
 LEN = 32
 DAMPING = 0.25
-STEPS = 16
+STEPS = 24
+LAG = 2
 MESH = pl.DeviceIdType.MESH
 VMEM_LIMIT = 60 * 1024 * 1024
 
@@ -157,10 +158,12 @@
                     self.out(m, h, 0, lambda copy: copy.wait_send())
 
 
-def turn_kernel(n_mp, n_dp, n_rep, fails, ids, counts, g_ref, a_ref, q_ref, basis_ref, u_out, r_out, q_out,
+def turn_kernel(n_mp, n_dp, n_rep, fails, ids, counts, g_ref, a_ref, q_ref, basis_hbm, u_out, r_out, q_out,
                 s_own, s_all, s_block, a_all, q_rows, q_cols, r_own, r_all, u_own, left, right,
                 s_send, s_recv, a_send, a_recv, qr_send, qr_recv, qc_send, qc_recv, r_send, r_recv,
-                ul_send, ul_recv, ur_send, ur_recv):
+                ul_send, ul_recv, ur_send, ur_recv, basis_ref, basis_sem):
+    load = pltpu.make_async_copy(basis_hbm, basis_ref, basis_sem)
+    load.start()
     z = lax.axis_index("mp")
     greet(z_links(n_mp) + x_links(n_dp) + core_links(n_rep))
     s = PlaneGather(s_own, s_all, s_send, s_recv, n_dp, n_rep)
@@ -194,6 +197,7 @@
     s.forward()
     qc.start()
     s.finish()
+    load.wait()
 
     def at(i):
         return pl.ds(pl.multiple_of(i * rows, rows), rows)
@@ -244,14 +248,14 @@
         r_own[...] = total.astype(jnp.bfloat16).reshape(r_own.shape)
         r.start()
 
-    @pl.loop(0, STEPS + n_mp - 1)
+    @pl.loop(0, STEPS + LAG * (n_mp - 1))
     def _(t):
         @pl.when((t < STEPS) & (t % per == 0))
         def _():
             turn(t // per)
 
-        i = t - z
-        j = t - (n_mp - 1 - z)
+        i = t - LAG * z
+        j = t - LAG * (n_mp - 1 - z)
 
         @pl.when((i >= 0) & (i < STEPS))
         def _():
@@ -305,8 +309,10 @@
     qr.finish()
 
 
-def back_kernel(n_mp, n_dp, n_rep, parts, d_ref, g_ref, q_ref, out_ref, back, held, part, other, across,
-                z_send, z_recv, c_send, c_recv, x_send, x_recv, o_send, o_recv):
+def back_kernel(n_mp, n_dp, n_rep, parts, d_ref, g_hbm, q_ref, out_ref, back, held, part, other, across,
+                z_send, z_recv, c_send, c_recv, x_send, x_recv, o_send, o_recv, g_ref, g_sem):
+    load = pltpu.make_async_copy(g_hbm, g_ref, g_sem)
+    load.start()
     z, x, c = lax.axis_index("mp"), lax.axis_index("dp"), lax.axis_index("rep")
     greet(z_links(n_mp) + x_links(n_dp) + core_links(n_rep))
     n = n_mp * parts
@@ -411,8 +417,9 @@
                 back[at, cols], q_ref[:, cols], (((1,), (1,)), ((), ())), preferred_element_type=jnp.float32)
 
     out_ref[...] = jnp.zeros_like(out_ref)
-
-    @pl.loop(0, n + 3)
+    load.wait()
+
+    @pl.loop(0, n + 2)
     def _(t):
         @pl.when(t < n)
         def _():
@@ -420,15 +427,15 @@
 
         @pl.when((t >= 1) & (t < n + 1))
         def _():
-            add_cores(t - 1)
-
-        @pl.when((t >= 2) & (t < n + 2))
-        def _():
-            add_chips(t - 2)
-
-        @pl.when(t >= 3)
-        def _():
-            finish(t - 3)
+            add_chips(t - 1)
+
+        @pl.when(t >= 2)
+        def _():
+            finish(t - 2)
+
+        @pl.when(t < n)
+        def _():
+            add_cores(t)
 
     @pl.loop(0, n)
     def _(p):
@@ -461,7 +468,7 @@
             jax.ShapeDtypeStruct((fails, LEN, features), bf16),
             jax.ShapeDtypeStruct((rows, n_mp * features), bf16),
         ),
-        in_specs=[smem, smem, vmem, vmem, vmem, vmem],
+        in_specs=[smem, smem, vmem, vmem, vmem, pl.BlockSpec(memory_space=pl.ANY)],
         out_specs=(vmem, vmem, vmem),
         scratch_shapes=[
             pltpu.VMEM((prompts, LEN, hidden), bf16),
@@ -475,7 +482,7 @@
             pltpu.VMEM((live, wide), bf16),
             pltpu.VMEM((live, wide), bf16),
             pltpu.VMEM((live, wide), bf16),
-        ] + plane_sems + line_sems + line_sems + plane_sems + plane_sems + [dma((STEPS,))] * 4,
+        ] + plane_sems + line_sems + line_sems + plane_sems + plane_sems + [dma((STEPS,))] * 4 + [pltpu.VMEM(basis_grad.shape, bf16), dma],
         compiler_params=pltpu.CompilerParams(
             collective_id=0, has_side_effects=True, vmem_limit_bytes=VMEM_LIMIT),
         name="turn_grads",
@@ -493,7 +500,7 @@
     return pl.pallas_call(
         functools.partial(back_kernel, n_mp, n_dp, n_rep, parts),
         out_shape=jax.ShapeDtypeStruct((hidden, rows), jnp.float32),
-        in_specs=[vmem, vmem, vmem],
+        in_specs=[vmem, pl.BlockSpec(memory_space=pl.ANY), vmem],
         out_specs=vmem,
         scratch_shapes=[
             pltpu.VMEM((hidden, n_mp * features), bf16),
@@ -505,6 +512,7 @@
             dma((n,)), dma((n,)),
             dma((n, n_dp - 1)), dma((n, n_dp - 1)),
             dma((n,)), dma((n,)),
+            pltpu.VMEM(basis_grad.shape, bf16), dma,
         ],
         compiler_params=pltpu.CompilerParams(
             collective_id=1, has_side_effects=True, vmem_limit_bytes=VMEM_LIMIT),

time: 306 us -> 284 us (0.928)
  Pallas kernels: 297 us -> 274 us
    pallas_call x1, Pallas kernels: 148 us -> 130 us  [shards(): pl.pallas_call(functools.partial(turn_kernel, n_mp, n_dp, n_rep, fails),...]
    pallas_call x1, Pallas kernels: 148 us -> 144 us  [shards(): pl.pallas_call(functools.partial(back_kernel, n_mp, n_dp, n_rep, parts),...]
where the time goes in v3:
time: 284 us; the launch traced here: 283 us
  Pallas kernels  274 us (96%)
  matrix products  4.91 us (2%)
  local copies, waits for them, and re-layouts  4.25 us (1%)
    pallas_call x1, Pallas kernels, shards(): pl.pallas_call(functools.partial(back_kernel, n_mp, n_dp, n_rep, parts),...  144 us
    pallas_call x1, Pallas kernels, shards(): pl.pallas_call(functools.partial(turn_kernel, n_mp, n_dp, n_rep, fails),...  130 us

profile of v3, /device:TPU:0, one launch (start us, length us, event | category | flops | bytes accessed | tf_op | source)
XLA Modules:
  0.0 283.4 jit_solution(3588961002260339222)
XLA Ops:
  0.0 0.0 copy-start
  0.0 130.2 %turn_grads.1 = (bf16[768,1792]{1,0:T(8,128)(2,1)}, bf16[24,32,512]{2,1,0:T(8,128)(2,1)}, bf16[512,2048]{1,0:T(8,128)(2,1)}) custom-call(s32[24]{0:T(128)} %ids.1, s32[8]{0:T(128)} %counts.1, bf16[8,32,1792]{2,1,0:T(8,128)(2,1)} %bitcast.4, bf16[256,512]{1,0:T(8,128)(2,1)} %a_ref.1, bf16[512,512]{1,0:T(8,128)(2,1)} %q_ref.1, bf16[1792,1792]{1,0:T(8,128)(2,1)} %g_hbm.1), custom_call_target="tpu_custom_call" | custom-call | tf_op jit(solution)/shard_map/turn_grads/pallas_call | solution.py:464
  130.2 0.0 copy-done
  130.2 4.9 %divide_convert_fusion.d_ref = bf16[1792,512]{1,0:T(8,128)(2,1)} fusion(f32[1792,512]{1,0:T(8,128)S(1)} %copy-done, bf16[768,1792]{1,0:T(8,128)(2,1)} %get-tuple-element.8, bf16[768,512]{1,0:T(8,128)(2,1)} %bitcast.5), kind=kOutput, calls=%fused_computation | convolution fusion | flops 1412038656 | bytes 9043968 | tf_op jit(solution)/shard_map/dot_general | solution.py:492
  135.1 144.0 %back_rotate.1 = f32[1792,512]{1,0:T(8,128)} custom-call(bf16[1792,512]{1,0:T(8,128)(2,1)} %divide_convert_fusion.d_ref, bf16[1792,1792]{1,0:T(8,128)(2,1)} %g_hbm.1, bf16[512,2048]{1,0:T(8,128)(2,1)} %get-tuple-element.10.q_ref), custom_call_target="tpu_custom_call" | custom-call | tf_op jit(solution)/shard_map/back_rotate/pallas_call | solution.py:500
  279.1 4.2 %copy.9 = f32[1792,512]{1,0:T(8,128)} copy(f32[1792,512]{1,0:T(8,128)} %back_rotate.1) | data formatting | bytes 7340032
Async XLA Ops:
  0.0 130.2 %copy-start = (f32[1792,512]{1,0:T(8,128)S(1)}, f32[1792,512]{1,0:T(8,128)}, u32[]{:S(2)}) copy-start(f32[1792,512]{1,0:T(8,128)} %param.11) | copy-start | bytes 11010052

commit v4 on v3

--- a/solution.py
+++ b/solution.py
@@ -11,6 +11,7 @@
 DAMPING = 0.25
 STEPS = 24
 LAG = 2
+PART = 128
 MESH = pl.DeviceIdType.MESH
 VMEM_LIMIT = 60 * 1024 * 1024
 
@@ -158,8 +159,8 @@
                     self.out(m, h, 0, lambda copy: copy.wait_send())
 
 
-def turn_kernel(n_mp, n_dp, n_rep, fails, ids, counts, g_ref, a_ref, q_ref, basis_hbm, u_out, r_out, q_out,
-                s_own, s_all, s_block, a_all, q_rows, q_cols, r_own, r_all, u_own, left, right,
+def turn_kernel(n_mp, n_dp, n_rep, fails, ids, counts, g_ref, a_ref, q_ref, basis_hbm, u_out, r_out, q_rows,
+                s_own, s_all, s_block, a_all, q_cols, r_own, r_all, u_own, left, right,
                 s_send, s_recv, a_send, a_recv, qr_send, qr_recv, qc_send, qc_recv, r_send, r_recv,
                 ul_send, ul_recv, ur_send, ur_recv, basis_ref, basis_sem):
     load = pltpu.make_async_copy(basis_hbm, basis_ref, basis_sem)
@@ -220,6 +221,10 @@
         def _():
             copy(buf, i, send, recv, way).start()
 
+    def total(i):
+        u_out[at(i), :] = (left[at(i), :].astype(jnp.float32) + right[at(i), :].astype(jnp.float32)
+                           - u_own[at(i), :].astype(jnp.float32)).astype(jnp.bfloat16)
+
     def turn(block):
         prompts = s_block.shape[0]
 
@@ -239,13 +244,12 @@
 
     def rotate():
         qc.finish()
-        total = jnp.zeros((a_ref.shape[0], width), jnp.float32)
-        total = lax.fori_loop(
+        product = lax.fori_loop(
             0, n_mp,
             lambda m, t: t + jnp.dot(a_all[m], q_cols[pl.ds(pl.multiple_of(m * depth, depth), depth), :],
                                      preferred_element_type=jnp.float32),
-            total)
-        r_own[...] = total.astype(jnp.bfloat16).reshape(r_own.shape)
+            jnp.zeros((a_ref.shape[0], width), jnp.float32))
+        r_own[...] = product.astype(jnp.bfloat16).reshape(r_own.shape)
         r.start()
 
     @pl.loop(0, STEPS + LAG * (n_mp - 1))
@@ -261,9 +265,17 @@
         def _():
             take(left, i, ul_send, ul_recv, 1, z == 0, z == n_mp - 1)
 
+            @pl.when(z > n_mp - 1 - z)
+            def _():
+                total(i)
+
         @pl.when((j >= 0) & (j < STEPS))
         def _():
             take(right, j, ur_send, ur_recv, -1, z == n_mp - 1, z == 0)
+
+            @pl.when(z <= n_mp - 1 - z)
+            def _():
+                total(j)
 
         for n in range(1, n_mp):
             @pl.when(t == (n - 1) * STEPS // (n_mp - 1))
@@ -284,9 +296,6 @@
 
     @pl.loop(0, STEPS)
     def _(i):
-        u_out[at(i), :] = (left[at(i), :].astype(jnp.float32) + right[at(i), :].astype(jnp.float32)
-                           - u_own[at(i), :].astype(jnp.float32)).astype(jnp.bfloat16)
-
         @pl.when(z < n_mp - 1)
         def _():
             copy(left, i, ul_send, ul_recv, 1).wait_send()
@@ -301,15 +310,11 @@
     def _(i):
         r_out[i] = r_all[ids[i]]
 
-    @pl.loop(0, n_mp)
-    def _(m):
-        q_out[:, pl.ds(pl.multiple_of(m * width, width), width)] = q_rows[m]
-
     a.finish()
     qr.finish()
 
 
-def back_kernel(n_mp, n_dp, n_rep, parts, d_ref, g_hbm, q_ref, out_ref, back, held, part, other, across,
+def back_kernel(n_mp, n_dp, n_rep, parts, u_ref, r_ref, e_ref, g_hbm, q_ref, out_ref, back, held, part, other, across,
                 z_send, z_recv, c_send, c_recv, x_send, x_recv, o_send, o_recv, g_ref, g_sem):
     load = pltpu.make_async_copy(g_hbm, g_ref, g_sem)
     load.start()
@@ -318,6 +323,7 @@
     n = n_mp * parts
     rows, width = held.shape[1], held.shape[2]
     half = rows // n_rep
+    deep = 256 if rows % 256 == 0 else rows
     tile = next(t for t in (256, 128, 64, 32, 16) if rows % t == 0)
     small = next(t for t in (128, 64, 32, 16) if half % t == 0)
     core = {"rep": 1 - c}
@@ -326,8 +332,17 @@
     line = LineGather(held, parts, z_send, z_recv, n_mp)
 
     for h in range(parts):
-        held[z * parts + h] = d_ref[:, h * width:(h + 1) * width]
-    line.start()
+        @pl.loop(0, held.shape[1] // deep)
+        def _(t):
+            at = pl.ds(pl.multiple_of(t * deep, deep), deep)
+            eigen_grad = lax.dot_general(
+                u_ref[:, at], r_ref[:, h * width:(h + 1) * width], (((0,), (0,)), ((), ())),
+                preferred_element_type=jnp.float32)
+            held[z * parts + h, at, :] = (
+                eigen_grad / (e_ref[at, h * width:(h + 1) * width] + DAMPING)).astype(jnp.bfloat16)
+
+        for way in (0, 1):
+            line.out(z, h, way, lambda copy: copy.start())
 
     low, high = z, n_mp - 1 - z
     near = jnp.minimum(low, high)
@@ -409,12 +424,13 @@
     def finish(p):
         out_copy(p, theirs).wait_recv()
         cols = columns(p)
+        m, h, _, _ = place(p)
 
         @pl.loop(0, rows // tile)
         def _(t):
             at = pl.ds(pl.multiple_of(t * tile, tile), tile)
             out_ref[at, :] += lax.dot_general(
-                back[at, cols], q_ref[:, cols], (((1,), (1,)), ((), ())), preferred_element_type=jnp.float32)
+                back[at, cols], q_ref[m, :, pl.ds(pl.multiple_of(h * width, width), width)], (((1,), (1,)), ((), ())), preferred_element_type=jnp.float32)
 
     out_ref[...] = jnp.zeros_like(out_ref)
     load.wait()
@@ -466,7 +482,7 @@
         out_shape=(
             jax.ShapeDtypeStruct((live, wide), bf16),
             jax.ShapeDtypeStruct((fails, LEN, features), bf16),
-            jax.ShapeDtypeStruct((rows, n_mp * features), bf16),
+            jax.ShapeDtypeStruct((n_mp, rows, features), bf16),
         ),
         in_specs=[smem, smem, vmem, vmem, vmem, pl.BlockSpec(memory_space=pl.ANY)],
         out_specs=(vmem, vmem, vmem),
@@ -475,7 +491,6 @@
             pltpu.VMEM((planes * prompts, LEN, hidden), bf16),
             pltpu.VMEM((fails // blocks, LEN, hidden), bf16),
             pltpu.VMEM((n_mp, tokens, features), bf16),
-            pltpu.VMEM((n_mp, rows, features), bf16),
             pltpu.VMEM((planes * rows, features), bf16),
             pltpu.VMEM((prompts, LEN, features), bf16),
             pltpu.VMEM((planes * prompts, LEN, features), bf16),
@@ -489,18 +504,14 @@
     )(fail_ids, token_counts, out_grads.reshape(prompts, LEN, hidden), activations, basis_act, basis_grad)
     rotated = rotated.reshape(live, features)
 
-    eigen_grad = lax.dot_general(
-        turned, rotated, (((0,), (0,)), ((), ())), preferred_element_type=jnp.float32)
-    damped = (eigen_grad / (eigen_values + DAMPING)).astype(bf16)
-
-    parts = max(1, features // 256)
+    parts = max(1, features // PART)
     width = features // parts
     n = n_mp * parts
     half = hidden // n_rep
     return pl.pallas_call(
         functools.partial(back_kernel, n_mp, n_dp, n_rep, parts),
         out_shape=jax.ShapeDtypeStruct((hidden, rows), jnp.float32),
-        in_specs=[vmem, pl.BlockSpec(memory_space=pl.ANY), vmem],
+        in_specs=[vmem, vmem, vmem, pl.BlockSpec(memory_space=pl.ANY), vmem],
         out_specs=vmem,
         scratch_shapes=[
             pltpu.VMEM((hidden, n_mp * features), bf16),
@@ -517,7 +528,7 @@
         compiler_params=pltpu.CompilerParams(
             collective_id=1, has_side_effects=True, vmem_limit_bytes=VMEM_LIMIT),
         name="back_rotate",
-    )(damped, basis_grad, basis_rows)
+    )(turned, rotated, eigen_values, basis_grad, basis_rows)
 
 
 def solution(mesh):

time: 284 us -> 292 us (1.028)
  Pallas kernels: 274 us -> 287 us
  matrix products: 4.91 us -> 0 us
    pallas_call x1, Pallas kernels: 144 us -> 159 us  [shards(): pl.pallas_call(functools.partial(back_kernel, n_mp, n_dp, n_rep, parts),...]
    dot_general x1 -> x0, matrix products: 4.91 us -> none  [shards(): lax.dot_general(turned, rotated, (((0,), (0,)), ((), ())), preferred_elem...]
where the time goes in v4:
time: 292 us
  Pallas kernels  287 us (98%)
  local copies, waits for them, and re-layouts  4.25 us (1%)
    pallas_call x1, Pallas kernels, shards(): pl.pallas_call(functools.partial(back_kernel, n_mp, n_dp, n_rep, parts),...  159 us
    pallas_call x1, Pallas kernels, shards(): pl.pallas_call(functools.partial(turn_kernel, n_mp, n_dp, n_rep, fails),...  129 us

profile of v4, /device:TPU:0, one launch (start us, length us, event | category | flops | bytes accessed | tf_op | source)
XLA Modules:
  0.0 291.7 jit_solution(17905995681427856218)
XLA Ops:
  0.0 128.9 %turn_grads.1 = (bf16[768,1792]{1,0:T(8,128)(2,1)}, bf16[24,32,512]{2,1,0:T(8,128)(2,1)}, bf16[4,512,512]{2,1,0:T(8,128)(2,1)}) custom-call(s32[24]{0:T(128)} %ids.1, s32[8]{0:T(128)} %counts.1, bf16[8,32,1792]{2,1,0:T(8,128)(2,1)} %bitcast.2, bf16[256,512]{1,0:T(8,128)(2,1)} %a_ref.1, bf16[512,512]{1,0:T(8,128)(2,1)} %q_ref.1, bf16[1792,1792]{1,0:T(8,128)(2,1)} %g_hbm.1), custom_call_target="tpu_custom_call" | custom-call | tf_op jit(solution)/shard_map/turn_grads/pallas_call | solution.py:480
  128.9 158.5 %back_rotate.1 = f32[1792,512]{1,0:T(8,128)} custom-call(bf16[768,1792]{1,0:T(8,128)(2,1)} %get-tuple-element.8.u_ref, bf16[768,512]{1,0:T(8,128)(2,1)} %bitcast.3, f32[1792,512]{1,0:T(8,128)} %e_ref.1, bf16[1792,1792]{1,0:T(8,128)(2,1)} %g_hbm.1, bf16[4,512,512]{2,1,0:T(8,128)(2,1)} %get-tuple-element.10.q_ref), custom_call_target="tpu_custom_call" | custom-call | tf_op jit(solution)/shard_map/back_rotate/pallas_call | solution.py:511
  287.5 4.2 %copy.9 = f32[1792,512]{1,0:T(8,128)} copy(f32[1792,512]{1,0:T(8,128)} %back_rotate.1) | data formatting | bytes 7340032

commit v5 on v4

--- a/solution.py
+++ b/solution.py
@@ -11,7 +11,6 @@
 DAMPING = 0.25
 STEPS = 24
 LAG = 2
-PART = 128
 MESH = pl.DeviceIdType.MESH
 VMEM_LIMIT = 60 * 1024 * 1024
 
@@ -278,7 +277,7 @@
                 total(j)
 
         for n in range(1, n_mp):
-            @pl.when(t == (n - 1) * STEPS // (n_mp - 1))
+            @pl.when(t == min((n - 1) * STEPS // 4, STEPS + LAG * (n_mp - 1) - 1))
             def _():
                 qr.step(n)
 
@@ -314,7 +313,7 @@
     qr.finish()
 
 
-def back_kernel(n_mp, n_dp, n_rep, parts, u_ref, r_ref, e_ref, g_hbm, q_ref, out_ref, back, held, part, other, across,
+def back_kernel(n_mp, n_dp, n_rep, parts, d_ref, g_hbm, q_ref, out_ref, back, held, part, other, across,
                 z_send, z_recv, c_send, c_recv, x_send, x_recv, o_send, o_recv, g_ref, g_sem):
     load = pltpu.make_async_copy(g_hbm, g_ref, g_sem)
     load.start()
@@ -323,7 +322,6 @@
     n = n_mp * parts
     rows, width = held.shape[1], held.shape[2]
     half = rows // n_rep
-    deep = 256 if rows % 256 == 0 else rows
     tile = next(t for t in (256, 128, 64, 32, 16) if rows % t == 0)
     small = next(t for t in (128, 64, 32, 16) if half % t == 0)
     core = {"rep": 1 - c}
@@ -332,17 +330,8 @@
     line = LineGather(held, parts, z_send, z_recv, n_mp)
 
     for h in range(parts):
-        @pl.loop(0, held.shape[1] // deep)
-        def _(t):
-            at = pl.ds(pl.multiple_of(t * deep, deep), deep)
-            eigen_grad = lax.dot_general(
-                u_ref[:, at], r_ref[:, h * width:(h + 1) * width], (((0,), (0,)), ((), ())),
-                preferred_element_type=jnp.float32)
-            held[z * parts + h, at, :] = (
-                eigen_grad / (e_ref[at, h * width:(h + 1) * width] + DAMPING)).astype(jnp.bfloat16)
-
-        for way in (0, 1):
-            line.out(z, h, way, lambda copy: copy.start())
+        held[z * parts + h] = d_ref[:, h * width:(h + 1) * width]
+    line.start()
 
     low, high = z, n_mp - 1 - z
     near = jnp.minimum(low, high)
@@ -504,14 +493,18 @@
     )(fail_ids, token_counts, out_grads.reshape(prompts, LEN, hidden), activations, basis_act, basis_grad)
     rotated = rotated.reshape(live, features)
 
-    parts = max(1, features // PART)
+    eigen_grad = lax.dot_general(
+        turned, rotated, (((0,), (0,)), ((), ())), preferred_element_type=jnp.float32)
+    damped = (eigen_grad / (eigen_values + DAMPING)).astype(bf16)
+
+    parts = max(1, features // 256)
     width = features // parts
     n = n_mp * parts
     half = hidden // n_rep
     return pl.pallas_call(
         functools.partial(back_kernel, n_mp, n_dp, n_rep, parts),
         out_shape=jax.ShapeDtypeStruct((hidden, rows), jnp.float32),
-        in_specs=[vmem, vmem, vmem, pl.BlockSpec(memory_space=pl.ANY), vmem],
+        in_specs=[vmem, pl.BlockSpec(memory_space=pl.ANY), vmem],
         out_specs=vmem,
         scratch_shapes=[
             pltpu.VMEM((hidden, n_mp * features), bf16),
@@ -528,7 +521,7 @@
         compiler_params=pltpu.CompilerParams(
             collective_id=1, has_side_effects=True, vmem_limit_bytes=VMEM_LIMIT),
         name="back_rotate",
-    )(turned, rotated, eigen_values, basis_grad, basis_rows)
+    )(damped, basis_grad, basis_rows)
 
 
 def solution(mesh):

time: 292 us -> 283 us (0.969)
  Pallas kernels: 287 us -> 273 us
  matrix products: 0 us -> 4.91 us
    pallas_call x1, Pallas kernels: 159 us -> 144 us  [shards(): pl.pallas_call(functools.partial(back_kernel, n_mp, n_dp, n_rep, parts),...]
    dot_general x0 -> x1, matrix products: none -> 4.91 us  [shards(): lax.dot_general(turned, rotated, (((0,), (0,)), ((), ())), preferred_elem...]
where the time goes in v5:
time: 283 us; the launch traced here: 282 us
  Pallas kernels  273 us (96%)
  matrix products  4.91 us (2%)
  local copies, waits for them, and re-layouts  4.25 us (2%)
    pallas_call x1, Pallas kernels, shards(): pl.pallas_call(functools.partial(back_kernel, n_mp, n_dp, n_rep, parts),...  144 us
    pallas_call x1, Pallas kernels, shards(): pl.pallas_call(functools.partial(turn_kernel, n_mp, n_dp, n_rep, fails),...  129 us

profile of v5, /device:TPU:0, one launch (start us, length us, event | category | flops | bytes accessed | tf_op | source)
XLA Modules:
  0.0 282.4 jit_solution(17865520551467266603)
XLA Ops:
  0.0 0.0 copy-start
  0.0 129.0 %turn_grads.1 = (bf16[768,1792]{1,0:T(8,128)(2,1)}, bf16[24,32,512]{2,1,0:T(8,128)(2,1)}, bf16[4,512,512]{2,1,0:T(8,128)(2,1)}) custom-call(s32[24]{0:T(128)} %ids.1, s32[8]{0:T(128)} %counts.1, bf16[8,32,1792]{2,1,0:T(8,128)(2,1)} %bitcast.4, bf16[256,512]{1,0:T(8,128)(2,1)} %a_ref.1, bf16[512,512]{1,0:T(8,128)(2,1)} %q_ref.1, bf16[1792,1792]{1,0:T(8,128)(2,1)} %g_hbm.1), custom_call_target="tpu_custom_call" | custom-call | tf_op jit(solution)/shard_map/turn_grads/pallas_call | solution.py:469
  129.0 0.0 copy-done
  129.0 4.9 %divide_convert_fusion.d_ref = bf16[1792,512]{1,0:T(8,128)(2,1)} fusion(f32[1792,512]{1,0:T(8,128)S(1)} %copy-done, bf16[768,1792]{1,0:T(8,128)(2,1)} %get-tuple-element.8, bf16[768,512]{1,0:T(8,128)(2,1)} %bitcast.5), kind=kOutput, calls=%fused_computation | convolution fusion | flops 1412038656 | bytes 9043968 | tf_op jit(solution)/shard_map/dot_general | solution.py:496
  133.9 144.2 %back_rotate.1 = f32[1792,512]{1,0:T(8,128)} custom-call(bf16[1792,512]{1,0:T(8,128)(2,1)} %divide_convert_fusion.d_ref, bf16[1792,1792]{1,0:T(8,128)(2,1)} %g_hbm.1, bf16[4,512,512]{2,1,0:T(8,128)(2,1)} %get-tuple-element.10.q_ref), custom_call_target="tpu_custom_call" | custom-call | tf_op jit(solution)/shard_map/back_rotate/pallas_call | solution.py:504
  278.2 4.2 %copy.9 = f32[1792,512]{1,0:T(8,128)} copy(f32[1792,512]{1,0:T(8,128)} %back_rotate.1) | data formatting | bytes 7340032
Async XLA Ops:
  0.0 129.0 %copy-start = (f32[1792,512]{1,0:T(8,128)S(1)}, f32[1792,512]{1,0:T(8,128)}, u32[]{:S(2)}) copy-start(f32[1792,512]{1,0:T(8,128)} %param.11) | copy-start | bytes 11010052
